TPU v7x, 256 devices: a whole 4x4x8 slice. The times are simulated.
256 devices in a mesh: seq: 64 (over z, x, core), head: 4 (over y).
Axes of the slice: x: 4, y: 4, z: 8, core: 2. Of those that a mesh axis runs over, the one named last changes fastest.
Arguments:
- queries: bfloat16 [4, 16384, 128], P('head', 'seq'), may hold values from -8 to 8
- keys: bfloat16 [4, 16384, 128], P('head', 'seq'), may hold values from -6 to 6
- state_b: bfloat16 [4, 16384, 128], P('head', 'seq'), may hold values from -6 to 6
- state_c: bfloat16 [4, 16384, 128], P('head', 'seq'), may hold values from -6 to 6
- decay: float32 [4, 16384], P('head', 'seq'), may hold values from -1 to 0, as said below
Outputs:
- grad_b: float32 [4, 16384, 128], P('head', 'seq')
- grad_c: float32 [4, 16384, 128], P('head', 'seq')
- grad_decay: float32 [4, 16384], P('head', 'seq')
- distance: float32 [], replicated
Inputs may be any that keep to these rules, and one draw needn't show every extreme that they name: decay is negative.
All inputs are finite; a program needn't handle non-finite values.
Results may differ from a plain program's by a relative error of at most 0.00096.
Values may be sent and summed in bfloat16 or wider, within the bound.
A program may use at most 128 MiB of HBM per device.

v0:
```python
import math

import jax
import jax.numpy as jnp
from jax import lax
from jax.sharding import PartitionSpec as P

floor_score = -1e30


def prefix(part, axis, combine, identity, reverse):
    count = lax.axis_size(axis)
    place = lax.axis_index(axis)
    ahead = count - 1 - place if reverse else place
    gathered = lax.all_gather(part, axis)
    state = jnp.zeros_like(part) + jnp.asarray(identity, part.dtype)

    def one(lap, state):
        source = count - 1 - lap if reverse else lap
        return combine(state, lax.dynamic_index_in_dim(gathered, source, 0, False))

    return lax.fori_loop(0, ahead, one, state)


def score_block(query_rows, key_rows):
    return jnp.dot(query_rows, key_rows.T, preferred_element_type=jnp.float32) / math.sqrt(
        query_rows.shape[1]
    )


def pair_block(scores, causal, log_total, cum_query, cum_key, output_rows, input_rows, weight):
    attention = jnp.where(causal, jnp.exp(scores - log_total[:, None]), 0.0)
    spread = jnp.where(
        causal, jnp.exp(jnp.minimum(cum_query[:, None] - cum_key[None, :], 0.0)), 0.0
    )
    student = (
        weight * spread * jnp.dot(output_rows, input_rows.T, preferred_element_type=jnp.float32)
    )
    misfit = student - attention
    return ((misfit * spread).astype(jnp.bfloat16), misfit)


def row_max_update(state_acc, query_rows, pos_query, key_rows, pos_key):
    running_max, denominator = state_acc
    scores = score_block(query_rows, key_rows)
    causal = pos_query[:, None] >= pos_key[None, :]
    new_max = jnp.maximum(running_max, jnp.max(jnp.where(causal, scores, floor_score), axis=1))
    fresh = jnp.sum(jnp.where(causal, jnp.exp(scores - new_max[:, None]), 0.0), axis=1)
    return (new_max, denominator * jnp.exp(running_max - new_max) + fresh)


def add_terms(earlier, later):
    return earlier + later


def local(queries, keys, state_b, state_c, decay):
    query_own = queries[0]
    input_own = state_b[0]
    output_own = state_c[0]
    shard_rows = query_own.shape[0]
    state_width = input_own.shape[1]
    devices = lax.axis_size("seq")
    total_rows = shard_rows * devices
    weight = 4.0 / total_rows
    row_first = lax.axis_index("seq") * shard_rows
    row_last = row_first + shard_rows - 1
    pos_query = row_first + jnp.arange(shard_rows, dtype=jnp.int32)
    local_cum = jnp.cumsum(decay[0])
    before = prefix(local_cum[-1:], "seq", add_terms, jnp.zeros((1,), jnp.float32), False)
    cum_own = local_cum + before[0]
    cum_all = lax.all_gather(cum_own[None], "seq", axis=1, tiled=True)
    start_max = (
        jnp.full((shard_rows,), floor_score, jnp.float32),
        jnp.zeros((shard_rows,), jnp.float32),
    )
    start_pairs = (jnp.zeros((shard_rows, state_width), jnp.float32), jnp.zeros((), jnp.float32))
    key_all, input_all = (
        lax.all_gather(keys, "seq", axis=1, tiled=True),
        lax.all_gather(state_b, "seq", axis=1, tiled=True),
    )
    block_rows = math.gcd(total_rows, 1024)
    block_count = row_last // block_rows + 1

    def scan_max(block_index, state_acc):
        begin_row = block_index * block_rows
        key_rows = lax.dynamic_slice_in_dim(key_all[0], begin_row, block_rows)
        pos_key = begin_row + jnp.arange(block_rows, dtype=jnp.int32)
        return row_max_update(state_acc, query_own, pos_query, key_rows, pos_key)

    running_max, denominator = lax.fori_loop(0, block_count, scan_max, start_max)
    log_total = running_max + jnp.log(denominator)

    def tile_at(begin_row):
        key_rows = lax.dynamic_slice_in_dim(key_all[0], begin_row, block_rows)
        input_rows = lax.dynamic_slice_in_dim(input_all[0], begin_row, block_rows)
        cum_key = lax.dynamic_slice_in_dim(cum_all[0], begin_row, block_rows)
        pos_key = begin_row + jnp.arange(block_rows, dtype=jnp.int32)
        scores = score_block(query_own, key_rows)
        causal = pos_query[:, None] >= pos_key[None, :]
        mixed_tile, misfit = pair_block(
            scores, causal, log_total, cum_own, cum_key, output_own, input_rows, weight
        )
        return (mixed_tile, misfit, input_rows)

    def scan_full(block_index, state_acc):
        begin_row = block_index * block_rows
        mixed_tile, misfit, input_rows = tile_at(begin_row)
        product = jnp.dot(mixed_tile.T, output_own, preferred_element_type=jnp.float32)
        current = lax.dynamic_slice_in_dim(state_acc[2], begin_row, block_rows)
        updated = lax.dynamic_update_slice_in_dim(state_acc[2], current + product, begin_row, 0)
        return (
            state_acc[0] + jnp.dot(mixed_tile, input_rows, preferred_element_type=jnp.float32),
            state_acc[1] + jnp.sum(misfit * misfit),
            updated,
        )

    start_full = (start_pairs[0], start_pairs[1], jnp.zeros((total_rows, state_width), jnp.float32))
    grad_out, square_sum, local_grad_full = lax.fori_loop(0, block_count, scan_full, start_full)
    log_total, grad_out, square_sum, grad_full = (log_total, grad_out, square_sum, local_grad_full)
    grad_in = lax.psum_scatter(grad_full, "seq", scatter_dimension=0, tiled=True)
    cum_gradient = jnp.sum(output_own.astype(jnp.float32) * grad_out, axis=1) - jnp.sum(
        input_own.astype(jnp.float32) * grad_in, axis=1
    )
    behind = jnp.flip(jnp.cumsum(jnp.flip(cum_gradient)))
    suffix_sum = prefix(behind[:1], "seq", add_terms, jnp.zeros((1,), jnp.float32), True)
    grad_decay = ((behind + suffix_sum[0]) / math.sqrt(total_rows))[None]
    head_count = lax.axis_size("head") * queries.shape[0]
    everything = lax.psum(square_sum, ("seq", "head"))
    distance = jnp.sqrt(everything / (head_count * total_rows))
    return (grad_in[None], grad_out[None], grad_decay, distance)


def solution(mesh):
    return jax.shard_map(
        local,
        mesh=mesh,
        in_specs=(
            P("head", "seq", None),
            P("head", "seq", None),
            P("head", "seq", None),
            P("head", "seq", None),
            P("head", "seq"),
        ),
        out_specs=(P("head", "seq", None), P("head", "seq", None), P("head", "seq"), P()),
        check_vma=False,
    )
```

profile of v0, /device:TPU:8, one launch (start us, length us, event | category | flops | bytes accessed | tf_op | source)
XLA Modules:
  0.0 772.7 jit_solution(17249205068558108466)
XLA Ops:
  7.2 0.7 all-gather.7.cloned.1.call-update
  7.9 0.7 all-gather.5.cloned.1.call-update
  8.7 1.0 reduce-window.16
  9.8 1.3 dynamic-slice.4
  11.3 0.8 slice_dynamic-update-slice_fusion.1
  12.1 131.7 %all-reduce = f32[64]{0:T(128)S(1)} all-reduce(f32[64]{0:T(128)S(1)} %slice_dynamic-update-slice_fusion.1), channel_id=2, replica_groups=mesh['seq'=64,'head'=4] {'seq'}, use_global_device_ids=true, to_apply=%add | all-reduce | flops 64 | bytes 512
  143.9 117.8 %all_gather.23 = f32[1,16384]{1,0:T(1,128)S(1)} all-gather(f32[1,256]{1,0:T(1,128)S(1)} %bitcast.90), channel_id=1, replica_groups=mesh['seq'=64,'head'=4] {'seq'}, dimensions={1}, use_global_device_ids=true | all-gather | bytes 66560 | tf_op jit(solution)/shard_map/all_gather | solution.py:71
  261.6 1.6 while.52
  261.7 1.3 fusion.46
  263.4 3.5 broadcast_in_dim.40
  266.9 7.6 while.53
  266.9 1.3 fusion.55
  268.3 2.1 multiply_reduce_fusion.3
  270.4 1.3 convolution_add_fusion.3
  272.3 2.1 fusion.56
  274.5 209.6 %psum.7 = f32[]{:T(128)} all-reduce(f32[]{:T(128)} %get-tuple-element.198), channel_id=1, replica_groups=mesh['seq'=64,'head'=4] {'seq','head'}, use_global_device_ids=true, to_apply=%region_18.19 | all-reduce | flops 1 | bytes 8 | tf_op jit(solution)/shard_map/psum | solution.py:128
  484.9 73.7 %reduce-scatter.2.cloned.1.call-done = f32[256,128]{1,0:T(8,128)} async-done(((f32[16384,128]{1,0:T(8,128)}), f32[256,128]{1,0:T(8,128)}) %reduce-scatter.2.cloned.1.call-update) | async-done | bytes 131088 | tf_op jit(solution)/shard_map/reduce_scatter | solution.py:120
  558.6 1.0 fusion.26
  560.4 0.8 slice_dynamic-update-slice_fusion
  561.2 124.0 %all-reduce.1 = f32[64]{0:T(128)S(1)} all-reduce(f32[64]{0:T(128)S(1)} %slice_dynamic-update-slice_fusion), channel_id=3, replica_groups=mesh['seq'=64,'head'=4] {'seq'}, use_global_device_ids=true, to_apply=%add.1 | all-reduce | flops 64 | bytes 512
  685.2 79.2 %while.51 = (s32[]{:T(128)}, f32[1]{0:T(128)}, s32[]{:T(128)}, f32[64,1]{0,1:T(1,128)S(1)}, s32[]{:T(128)}, /*index=5*/s32[]{:T(128)}, s32[]{:T(128)}, s32[]{:T(128)}) while((s32[]{:T(128)}, f32[1]{0:T(128)}, s32[]{:T(128)}, f32[64,1]{0,1:T(1,128)S(1)}, s32[]{:T(128)}, /*index=5*/s32[]{:T(128)}, s32[]{:T(128)}, s32[]{:T(128)}) %tuple.103), condition=%wide.region_17.18_spmd, body=%wide.region_16.17_spmd.sunk | while | flops 7 | bytes 163 | solution.py:22
  685.2 0.6 constant_dynamic-slice_fusion.7
  687.8 0.6 constant_dynamic-slice_fusion.7
  692.8 0.6 constant_dynamic-slice_fusion.7
  706.6 0.6 constant_dynamic-slice_fusion.7
  711.7 0.6 constant_dynamic-slice_fusion.7
  716.7 0.6 constant_dynamic-slice_fusion.7
  730.5 0.6 constant_dynamic-slice_fusion.7
  735.6 0.6 constant_dynamic-slice_fusion.7
  740.6 0.6 constant_dynamic-slice_fusion.7
  754.4 0.6 constant_dynamic-slice_fusion.7
  759.5 0.6 constant_dynamic-slice_fusion.7
  (98 shorter events, 32.8 us)
Async XLA Ops:
  7.2 254.5 %all-gather.7.cloned.1.call-start = ((), (), s32[]{:S(2)}) async-start(), calls=%async_computation.2 | async-start | bytes 4259840 | tf_op jit(solution)/shard_map/all_gather | solution.py:78
  7.9 255.4 %all-gather.5.cloned.1.call-start = ((), (), s32[]{:S(2)}) async-start(), calls=%async_computation.1 | async-start | bytes 4259840 | tf_op jit(solution)/shard_map/all_gather | solution.py:79
  8.7 549.9 %reduce-scatter.2.cloned.1.call-start = ((), (), s32[]{:S(2)}) async-start(), calls=%async_computation.3 | async-start | bytes 8519680 | tf_op jit(solution)/shard_map/reduce_scatter | solution.py:120
  263.4 3.5 copy-start.1
  263.4 3.5 copy-start.3
  274.5 210.3 %copy-start = (f32[256,128]{1,0:T(8,128)}, f32[256,128]{1,0:T(8,128)S(1)}, u32[]{:S(2)}) copy-start(f32[256,128]{1,0:T(8,128)S(1)} %get-tuple-element.196) | copy-start | bytes 393220
  274.5 284.1 %copy-start.2 = (bf16[1,256,128]{2,1,0:T(8,128)(2,1)S(1)}, bf16[1,256,128]{2,1,0:T(8,128)(2,1)}, u32[]{:S(2)}) copy-start(bf16[1,256,128]{2,1,0:T(8,128)(2,1)} %param.15) | copy-start | bytes 196612
Sparse Core Ops, SparseCore 0:
  10.8 81.8 all-gather.6
  95.4 76.2 all-gather.4
  274.6 283.9 reduce-scatter.1
where the time goes:
time: 776 us; the launch traced here: 773 us
  blocking collectives  583 us (75%)
  waiting for transfers between devices  75.1 us (10%)
  local copies, waits for them, and re-layouts  43.8 us (6%)
  loops' own time  43.1 us (6%)
  between operations  15.7 us (2%)
  matrix products  8.2 us (1%)
    unnamed x2, blocking collectives  256 us
    psum x1, blocking collectives, local(): everything = lax.psum(square_sum, ('seq', 'head'))  210 us
    all_gather x1, blocking collectives, local(): cum_all = lax.all_gather(cum_own[None], 'seq', axis=1, tiled=True)  118 us
    reduce_scatter x1, waiting for transfers between devices, local(): lax.psum_scatter(grad_full, 'seq', scatter_dimension=0, tiled=True)  73.7 us
    another operation x2, loops' own time, prefix(): return lax.fori_loop(0, ahead, one, state)  42.4 us
    dynamic_slice x63, local copies, waits for them, and re-layouts, one(): return combine(state, lax.dynamic_index_in_dim(gathered, source, 0, False))  36.9 us
  transfers between devices with their start and end apart: 3, of which 1 were waited for; matrix products, arithmetic and copies ran while one was open for 1% of the time, Pallas kernels for 0%

commit v1 on v0

v1 whole, which is shorter than its diff:
```python
import math

import jax
import jax.numpy as jnp
from jax import lax
from jax.experimental import pallas as pl
from jax.experimental.pallas import tpu as pltpu
from jax.sharding import PartitionSpec as P

SIDE = 8
STEPS = (1, -2, 3, 4)
UNITS = len(STEPS)
SLOTS = SIDE + UNITS
LOG2E = math.log2(math.e)
FLOOR = -1e30
F32 = jnp.float32
BF16 = jnp.bfloat16


def dot_nt(a, b):
    return lax.dot_general(a, b, (((1,), (1,)), ((), ())), preferred_element_type=F32)


def dot_nn(a, b):
    return lax.dot_general(a, b, (((1,), (0,)), ((), ())), preferred_element_type=F32)


def running(x, reverse):
    width = x.shape[-1]
    lane = lax.broadcasted_iota(jnp.int32, x.shape, x.ndim - 1)
    step = 1
    while step < width:
        if reverse:
            x = x + jnp.where(lane < width - step, pltpu.roll(x, width - step, x.ndim - 1), 0.0)
        else:
            x = x + jnp.where(lane >= step, pltpu.roll(x, step, x.ndim - 1), 0.0)
        step *= 2
    return x


def spread_lanes(column, width):
    return jnp.broadcast_to(column, (column.shape[0], width))


def kernel(
    heads, total_rows,
    q_hbm, k_hbm, b_hbm, c_hbm, dec_hbm,
    gb_out, gc_out, gd_out, dist_out,
    QK, CB, BT, DEC, GCOL, CUMCOL, E, MB, ST, RST, RSTX, LB, CUMV, REFV, D1, D2,
    GB, GCT, RGB, RGCT, RXB, RXC, SQ, T1, T2, T3,
    load_sem, qk_send, qk_recv, qkx_send, qkx_recv, cb_send, cb_recv, cbx_send, cbx_recv,
    d1_send, d1_recv, d2_send, d2_recv, st_send, st_recv, stx_send, stx_recv,
    l_send, l_recv, lx_send, lx_recv, gb_send, gb_recv, gc_send, gc_recv, gx_send, gx_recv,
    t1_send, t1_recv, t2_send, t2_recv, t3_send, t3_recv,
):
    n = lax.axis_index("seq")
    h = lax.axis_index("head")
    z = lax.div(n, SIDE)
    b = lax.rem(n, SIDE)
    R = q_hbm.shape[0]
    weight = 4.0 / total_rows
    scale2 = LOG2E / math.sqrt(q_hbm.shape[1])

    def mate(o):
        return {"seq": z * SIDE + o}

    def other(row):
        return {"seq": row * SIDE + b}

    def send(src, dst, ssem, rsem, where):
        pltpu.make_async_remote_copy(src, dst, ssem, rsem, device_id=where).start()

    def got(ref, ssem, rsem):
        pltpu.make_async_remote_copy(ref, ref, ssem, rsem, device_id=mate(b)).wait_recv()

    def sent(ref, ssem, rsem):
        pltpu.make_async_remote_copy(ref, ref, ssem, rsem, device_id=mate(b)).wait_send()

    def around(t):
        return lax.rem(b + t, SIDE)

    def row_of(u):
        return lax.rem(z + STEPS[u] + SIDE, SIDE)

    def holder(u):
        return lax.rem(z - STEPS[u] + SIDE, SIDE)

    def each_mate(body):
        def one(t, carry):
            body(lax.rem(b + t, SIDE))
            return carry

        lax.fori_loop(1, SIDE, one, 0)

    def each_row(body):
        def one(t, carry):
            body(lax.rem(z + t, SIDE))
            return carry

        lax.fori_loop(1, SIDE, one, 0)

    loads = [
        pltpu.make_async_copy(dec_hbm, DEC, load_sem.at[0]),
        pltpu.make_async_copy(q_hbm, QK.at[2 * b], load_sem.at[1]),
        pltpu.make_async_copy(k_hbm, QK.at[2 * b + 1], load_sem.at[2]),
        pltpu.make_async_copy(b_hbm, CB.at[2 * b + 1], load_sem.at[3]),
        pltpu.make_async_copy(c_hbm, CB.at[2 * b], load_sem.at[4]),
    ]
    for one in loads:
        one.start()
    barrier = pltpu.get_barrier_semaphore()
    each_mate(lambda o: pl.semaphore_signal(barrier, inc=1, device_id=mate(o)))
    each_row(lambda r: pl.semaphore_signal(barrier, inc=1, device_id=other(r)))
    for step in range(1, heads):
        pl.semaphore_signal(barrier, inc=1, device_id={"head": lax.rem(h + step, heads)})

    loads[0].wait()
    own_cum = running(DEC[...] * LOG2E, False)
    own_total = jnp.broadcast_to(own_cum[:, R - 1 : R], (1, R))
    D1[b] = jnp.broadcast_to(own_cum, (8, R))
    cum_col = jnp.broadcast_to(own_cum, (128, R)).T
    CUMCOL[...] = cum_col

    def columns(cum):
        column = jnp.broadcast_to(cum, (128, R)).T
        return jnp.exp2(jnp.minimum(column[R - 1 : R, :] - column, 0.0))

    for one in loads[1:]:
        one.wait()
    pl.semaphore_wait(barrier, 2 * (SIDE - 1) + heads - 1)

    each_mate(lambda o: send(D1.at[b], D1.at[b], d1_send.at[o], d1_recv.at[b], mate(o)))
    for u in range(UNITS):
        mine = 2 * b + jnp.where(z > holder(u), 0, 1)
        send(QK.at[mine], QK.at[2 * SIDE + u], qkx_send.at[u], qkx_recv.at[u], other(holder(u)))
    each_mate(lambda o: send(QK.at[pl.ds(2 * b, 2)], QK.at[pl.ds(2 * b, 2)], qk_send.at[o], qk_recv.at[b], mate(o)))
    for u in range(UNITS):
        mine = 2 * b + jnp.where(z > holder(u), 0, 1)
        send(CB.at[mine], CB.at[2 * SIDE + u], cbx_send.at[u], cbx_recv.at[u], other(holder(u)))
    each_mate(lambda o: send(CB.at[pl.ds(2 * b, 2)], CB.at[pl.ds(2 * b, 2)], cb_send.at[o], cb_recv.at[b], mate(o)))

    def clear(s, carry):
        GB[s] = jnp.zeros((R, 128), F32)
        GCT[s] = jnp.zeros((128, R), F32)
        ST[s, 0:1, :] = jnp.full((1, R), FLOOR, F32)
        ST[s, 1:2, :] = jnp.zeros((1, R), F32)
        return carry

    lax.fori_loop(0, SLOTS, clear, 0)
    SQ[...] = jnp.zeros_like(SQ)

    each_mate(lambda o: got(D1.at[o], d1_send.at[o], d1_recv.at[o]))
    before = jnp.zeros((1, R), F32)
    total = jnp.zeros((1, R), F32)
    starts = []
    for o in range(SIDE):
        part = jnp.broadcast_to(D1[o, 0:1, R - 1 : R], (1, R))
        starts.append(total)
        before = before + jnp.where(o < b, part, 0.0)
        total = total + part
    D2[z, 0:1, :] = own_cum
    D2[z, 1:2, :] = before
    D2[z, 2:3, :] = total
    each_row(lambda r: send(D2.at[z], D2.at[z], d2_send.at[r], d2_recv.at[z], other(r)))

    jj = lax.broadcasted_iota(jnp.int32, (R, R), 0)
    ii = lax.broadcasted_iota(jnp.int32, (R, R), 1)

    def note(s, m, l):
        old_m = ST[s, 0:1, :]
        old_l = ST[s, 1:2, :]
        new_m = jnp.maximum(old_m, m)
        ST[s, 0:1, :] = new_m
        ST[s, 1:2, :] = old_l * jnp.exp2(old_m - new_m) + l * jnp.exp2(m - new_m)

    def first(ri, ci, e, rs):
        s = dot_nt(QK[ci], QK[ri]) * scale2
        m = jnp.max(s, axis=0, keepdims=True)
        p = jnp.exp2(s - m)
        E[e] = p.astype(BF16)
        MB[e] = m
        note(rs, m, jnp.sum(p, axis=0, keepdims=True))

    own_e = UNITS * SIDE
    s = jnp.where(jj <= ii, dot_nt(QK[2 * b + 1], QK[2 * b]) * scale2, FLOOR)
    m = jnp.max(s, axis=0, keepdims=True)
    p = jnp.where(jj <= ii, jnp.exp2(s - m), 0.0)
    E[own_e] = p.astype(BF16)
    MB[own_e] = m
    note(b, m, jnp.sum(p, axis=0, keepdims=True))

    def pair(t):
        o = around(t)
        return jnp.maximum(b, o), jnp.minimum(b, o)

    def in_row(t, carry):
        o = around(t)
        got(QK.at[pl.ds(2 * o, 2)], qk_send.at[o], qk_recv.at[o])

        @pl.when(jnp.logical_or(t < SIDE // 2, jnp.logical_and(t == SIDE // 2, b < SIDE // 2)))
        def _():
            hi, lo = pair(t)
            first(2 * hi, 2 * lo + 1, own_e + t, hi)

        return carry

    lax.fori_loop(1, SIDE, in_row, 0)

    def span(u):
        if STEPS[u] * 2 == SIDE:
            return jnp.where(z < SIDE // 2, 0, 1), SIDE // 2
        return 0, SIDE

    def places(u, o):
        up = row_of(u) > z
        ri = jnp.where(up, 2 * SIDE + u, 2 * o)
        ci = jnp.where(up, 2 * o + 1, 2 * SIDE + u)
        rs = jnp.where(up, SIDE + u, o)
        cs = jnp.where(up, o, SIDE + u)
        return ri, ci, rs, cs

    group = 2
    for u in range(UNITS):
        got(QK.at[2 * SIDE + u], qkx_send.at[u], qkx_recv.at[u])
        begin, count = span(u)

        def unit_first(k, carry, u=u, begin=begin):
            for g in range(group):
                t = k * group + g
                ri, ci, rs, cs = places(u, around(begin + t))
                first(ri, ci, u * SIDE + t, rs)
            return carry

        lax.fori_loop(0, count // group, unit_first, 0)

    for u in range(UNITS):
        send(ST.at[SIDE + u], RSTX.at[u], stx_send.at[u], stx_recv.at[u], other(row_of(u)))
    each_mate(lambda o: send(ST.at[o], RST.at[b], st_send.at[o], st_recv.at[b], mate(o)))

    each_row(lambda r: got(D2.at[r], d2_send.at[r], d2_recv.at[r]))
    row_start = jnp.zeros((1, R), F32)
    row_starts = []
    for r in range(SIDE):
        row_starts.append(row_start)
        row_start = row_start + D2[r, 2:3, :]
    own_start = jnp.zeros((1, R), F32)
    for r in range(SIDE):
        own_start = jnp.where(z == r, row_starts[r], own_start)
    for o in range(SIDE):
        cum = D1[o, 0:1, :] + (starts[o] + own_start)
        CUMV[o] = cum
        REFV[o] = jnp.broadcast_to(cum[:, R - 1 : R], (1, R))
    for u in range(UNITS):
        r = row_of(u)
        start = jnp.zeros((1, R), F32)
        for k in range(SIDE):
            start = jnp.where(r == k, row_starts[k], start)
        cum = D2[r, 0:1, :] + (D2[r, 1:2, :] + start)
        CUMV[SIDE + u] = cum
        REFV[SIDE + u] = jnp.broadcast_to(cum[:, R - 1 : R], (1, R))

    def factors(o):
        GCOL[o] = columns(D1[o, 0:1, :])

    factors(b)
    each_mate(factors)
    for u in range(UNITS):
        GCOL[SIDE + u] = columns(D2[row_of(u), 0:1, :])

    BT[b] = CB[2 * b + 1].astype(F32).T.astype(BF16)

    def arrive(o):
        got(CB.at[pl.ds(2 * o, 2)], cb_send.at[o], cb_recv.at[o])
        BT[o] = CB[2 * o + 1].astype(F32).T.astype(BF16)

    each_mate(arrive)
    for u in range(UNITS):
        got(CB.at[2 * SIDE + u], cbx_send.at[u], cbx_recv.at[u])
        BT[SIDE + u] = CB[2 * SIDE + u].astype(F32).T.astype(BF16)

    def add_stats(ref, s, state):
        old_m, old_l = state
        m = ref[s, 0:1, :]
        new_m = jnp.maximum(old_m, m)
        return new_m, old_l * jnp.exp2(old_m - new_m) + ref[s, 1:2, :] * jnp.exp2(m - new_m)

    state = (ST[b, 0:1, :], ST[b, 1:2, :])
    each_mate(lambda o: got(RST.at[o], st_send.at[o], st_recv.at[o]))
    for t in range(1, SIDE):
        state = add_stats(RST, around(t), state)
    for u in range(UNITS):
        got(RSTX.at[u], stx_send.at[u], stx_recv.at[u])
        state = add_stats(RSTX, u, state)
    LB[b] = jnp.broadcast_to(state[0] + jnp.log2(state[1]), (8, R))
    for u in range(UNITS):
        send(LB.at[b], LB.at[SIDE + u], lx_send.at[u], lx_recv.at[u], other(holder(u)))
    each_mate(lambda o: send(LB.at[b], LB.at[b], l_send.at[o], l_recv.at[b], mate(o)))

    def square(x):
        y = x * x
        SQ[...] += jnp.sum(y.reshape(R // 8, 8, R), axis=0)

    def wide(column):
        return jnp.concatenate([column] * (R // 128), axis=1)

    def second(ri, ci, rs, cs, e):
        a = jnp.exp2(jnp.minimum(CUMV[rs] - REFV[cs], 0.0))
        f = jnp.exp2(MB[e] - LB[rs, 0:1, :])
        apart = wide(GCOL[cs]) * a
        misfit = dot_nt(CB[ci], CB[ri]) * (apart * weight) - E[e].astype(F32) * f
        square(misfit)
        mixed = (misfit * apart).astype(BF16)
        GB[cs] += dot_nn(mixed, CB[ri])
        GCT[rs] += dot_nn(BT[cs], mixed)

    causal = jj <= ii
    apart = jnp.exp2(jnp.minimum(own_cum - wide(CUMCOL[...]), 0.0))
    spread = jnp.where(causal, apart, 0.0)
    f = jnp.exp2(MB[own_e] - LB[b, 0:1, :])
    misfit = dot_nt(CB[2 * b + 1], CB[2 * b]) * (weight * spread) - E[own_e].astype(F32) * f
    square(misfit)
    mixed = (misfit * spread).astype(BF16)
    GB[b] += dot_nn(mixed, CB[2 * b])
    GCT[b] += dot_nn(BT[b], mixed)

    each_mate(lambda o: got(LB.at[o], l_send.at[o], l_recv.at[o]))
    for u in reversed(range(UNITS)):
        got(LB.at[SIDE + u], lx_send.at[u], lx_recv.at[u])
        begin, count = span(u)

        def unit_second(k, carry, u=u, begin=begin):
            for g in range(group):
                t = k * group + g
                ri, ci, rs, cs = places(u, around(begin + t))
                second(ri, ci, rs, cs, u * SIDE + t)
            return carry

        lax.fori_loop(0, count // group, unit_second, 0)
        up = row_of(u) > z

        @pl.when(up)
        def _(u=u):
            send(GCT.at[SIDE + u], RXC.at[u], gx_send.at[u], gx_recv.at[u], other(row_of(u)))

        @pl.when(jnp.logical_not(up))
        def _(u=u):
            send(GB.at[SIDE + u], RXB.at[u], gx_send.at[u], gx_recv.at[u], other(row_of(u)))

    def in_row_second(t, carry):
        @pl.when(jnp.logical_or(t < SIDE // 2, jnp.logical_and(t == SIDE // 2, b < SIDE // 2)))
        def _():
            hi, lo = pair(t)
            second(2 * hi, 2 * lo + 1, hi, lo, own_e + t)

        o = around(t)
        send(GB.at[o], RGB.at[b], gb_send.at[o], gb_recv.at[b], mate(o))
        send(GCT.at[o], RGCT.at[b], gc_send.at[o], gc_recv.at[b], mate(o))
        return carry

    lax.fori_loop(1, SIDE, in_row_second, 0)

    sq = jnp.sum(jnp.sum(SQ[...], axis=0, keepdims=True), axis=1, keepdims=True)
    T1[b, 1:2, :] = jnp.broadcast_to(sq, (1, R))

    for u in range(UNITS):

        @pl.when(z > holder(u))
        def _(u=u):
            got(RXC.at[u], gx_send.at[u], gx_recv.at[u])
            GCT[b] += RXC[u]

        @pl.when(z < holder(u))
        def _(u=u):
            got(RXB.at[u], gx_send.at[u], gx_recv.at[u])
            GB[b] += RXB[u]

    def add_mate(o):
        got(RGB.at[o], gb_send.at[o], gb_recv.at[o])
        GB[b] += RGB[o]
        got(RGCT.at[o], gc_send.at[o], gc_recv.at[o])
        GCT[b] += RGCT[o]

    each_mate(add_mate)
    grad_c = GCT[b].T
    grad_b = GB[b]
    gc_out[...] = grad_c
    gb_out[...] = grad_b
    flow = CB[2 * b].astype(F32) * grad_c - CB[2 * b + 1].astype(F32) * grad_b
    flow = jnp.sum(flow.T, axis=0, keepdims=True)
    behind = running(flow, True)
    T1[b, 0:1, :] = jnp.broadcast_to(behind[:, 0:1], (1, R))
    each_mate(lambda o: send(T1.at[b], T1.at[b], t1_send.at[o], t1_recv.at[b], mate(o)))
    each_mate(lambda o: got(T1.at[o], t1_send.at[o], t1_recv.at[o]))
    later = jnp.zeros((1, R), F32)
    row_flow = jnp.zeros((1, R), F32)
    row_sq = jnp.zeros((1, R), F32)
    for o in range(SIDE):
        later = later + jnp.where(o > b, T1[o, 0:1, :], 0.0)
        row_flow = row_flow + T1[o, 0:1, :]
        row_sq = row_sq + T1[o, 1:2, :]
    T2[z, 0:1, :] = row_flow
    T2[z, 1:2, :] = row_sq
    each_row(lambda r: send(T2.at[z], T2.at[z], t2_send.at[r], t2_recv.at[z], other(r)))
    each_row(lambda r: got(T2.at[r], t2_send.at[r], t2_recv.at[r]))
    head_sq = jnp.zeros((1, R), F32)
    for r in range(SIDE):
        later = later + jnp.where(r > z, T2[r, 0:1, :], 0.0)
        head_sq = head_sq + T2[r, 1:2, :]
    T3[h, 0:1, :] = head_sq
    for step in range(1, heads):
        to = lax.rem(h + step, heads)
        send(T3.at[h], T3.at[h], t3_send.at[to], t3_recv.at[h], {"head": to})
    gd_out[...] = (behind + later) * (1.0 / math.sqrt(total_rows))
    for step in range(1, heads):
        o = lax.rem(h + step, heads)
        got(T3.at[o], t3_send.at[o], t3_recv.at[o])
    everything = jnp.zeros((1, R), F32)
    for k in range(heads):
        everything = everything + T3[k, 0:1, :]
    dist_out[...] = jnp.sqrt(everything[:, :128] / (heads * total_rows))

    def drain(o):
        sent(D1.at[b], d1_send.at[o], d1_recv.at[b])
        sent(QK.at[pl.ds(2 * b, 2)], qk_send.at[o], qk_recv.at[b])
        sent(CB.at[pl.ds(2 * b, 2)], cb_send.at[o], cb_recv.at[b])
        sent(ST.at[o], st_send.at[o], st_recv.at[b])
        sent(LB.at[b], l_send.at[o], l_recv.at[b])
        sent(GB.at[o], gb_send.at[o], gb_recv.at[b])
        sent(GCT.at[o], gc_send.at[o], gc_recv.at[b])
        sent(T1.at[b], t1_send.at[o], t1_recv.at[b])

    each_mate(drain)

    def drain_row(r):
        sent(D2.at[z], d2_send.at[r], d2_recv.at[z])
        sent(T2.at[z], t2_send.at[r], t2_recv.at[z])

    each_row(drain_row)
    for step in range(1, heads):
        to = lax.rem(h + step, heads)
        sent(T3.at[h], t3_send.at[to], t3_recv.at[h])
    for u in range(UNITS):
        mine = 2 * b + jnp.where(z > holder(u), 0, 1)
        sent(QK.at[mine], qkx_send.at[u], qkx_recv.at[u])
        sent(CB.at[mine], cbx_send.at[u], cbx_recv.at[u])
        sent(ST.at[SIDE + u], stx_send.at[u], stx_recv.at[u])
        sent(LB.at[b], lx_send.at[u], lx_recv.at[u])
        up = row_of(u) > z

        @pl.when(up)
        def _(u=u):
            sent(GCT.at[SIDE + u], gx_send.at[u], gx_recv.at[u])

        @pl.when(jnp.logical_not(up))
        def _(u=u):
            sent(GB.at[SIDE + u], gx_send.at[u], gx_recv.at[u])


def local(queries, keys, state_b, state_c, decay):
    rows, width = queries.shape[1:]
    devices = lax.axis_size("seq")
    heads = lax.axis_size("head")
    total_rows = rows * devices
    assert devices == SIDE * SIDE and width == 128 and rows % 128 == 0
    blocks = UNITS * SIDE + SIDE // 2 + 1

    def vm(*shape, dtype=F32):
        return pltpu.VMEM(shape, dtype)

    def sems(*shape):
        return pltpu.SemaphoreType.DMA(shape)

    scratch = [
        vm(2 * SIDE + UNITS, rows, width, dtype=BF16),
        vm(2 * SIDE + UNITS, rows, width, dtype=BF16),
        vm(SLOTS, width, rows, dtype=BF16),
        vm(1, rows),
        vm(SLOTS, rows, width),
        vm(rows, width),
        vm(blocks, rows, rows, dtype=BF16),
        vm(blocks, 1, rows),
        vm(SLOTS, 8, rows),
        vm(SIDE, 8, rows),
        vm(UNITS, 8, rows),
        vm(SLOTS, 8, rows),
        vm(SLOTS, 1, rows),
        vm(SLOTS, 1, rows),
        vm(SIDE, 8, rows),
        vm(SIDE, 8, rows),
        vm(SLOTS, rows, width),
        vm(SLOTS, width, rows),
        vm(SIDE, rows, width),
        vm(SIDE, width, rows),
        vm(UNITS, rows, width),
        vm(UNITS, width, rows),
        vm(8, rows),
        vm(SIDE, 8, rows),
        vm(SIDE, 8, rows),
        vm(heads, 8, rows),
        sems(5),
        sems(SIDE), sems(SIDE), sems(UNITS), sems(UNITS),
        sems(SIDE), sems(SIDE), sems(UNITS), sems(UNITS),
        sems(SIDE), sems(SIDE), sems(SIDE), sems(SIDE),
        sems(SIDE), sems(SIDE), sems(UNITS), sems(UNITS),
        sems(SIDE), sems(SIDE), sems(UNITS), sems(UNITS),
        sems(SIDE), sems(SIDE), sems(SIDE), sems(SIDE), sems(UNITS), sems(UNITS),
        sems(SIDE), sems(SIDE), sems(SIDE), sems(SIDE), sems(heads), sems(heads),
    ]

    def body(*refs):
        kernel(heads, total_rows, *refs)

    anywhere = pl.BlockSpec(memory_space=pl.ANY)
    inside = pl.BlockSpec(memory_space=pltpu.VMEM)
    grad_b, grad_c, grad_decay, distance = pl.pallas_call(
        body,
        out_shape=(
            jax.ShapeDtypeStruct((rows, width), F32),
            jax.ShapeDtypeStruct((rows, width), F32),
            jax.ShapeDtypeStruct((1, rows), F32),
            jax.ShapeDtypeStruct((1, 128), F32),
        ),
        in_specs=[anywhere] * 5,
        out_specs=(inside,) * 4,
        scratch_shapes=scratch,
        compiler_params=pltpu.CompilerParams(
            collective_id=0, has_side_effects=True, vmem_limit_bytes=44 * 1024 * 1024
        ),
    )(queries[0], keys[0], state_b[0], state_c[0], decay)
    return grad_b[None], grad_c[None], grad_decay, distance[0, 0]


def solution(mesh):
    return jax.shard_map(
        local,
        mesh=mesh,
        in_specs=(
            P("head", "seq", None),
            P("head", "seq", None),
            P("head", "seq", None),
            P("head", "seq", None),
            P("head", "seq"),
        ),
        out_specs=(P("head", "seq", None), P("head", "seq", None), P("head", "seq"), P()),
        check_vma=False,
    )
```

time: 776 us -> 97.5 us (0.13)
  blocking collectives: 583 us -> 0 us
  Pallas kernels: 0 us -> 89.5 us
  waiting for transfers between devices: 75.1 us -> 0 us
  loops' own time: 43.1 us -> 0 us
  local copies, waits for them, and re-layouts: 43.8 us -> 5.9 us
  between operations: 15.7 us -> 1.82 us
  matrix products: 8.2 us -> 0 us
    unnamed x2 -> x0, blocking collectives: 256 us -> none
    psum x1 -> x0, blocking collectives: 210 us -> none  [local(): everything = lax.psum(square_sum, ('seq', 'head'))]
    all_gather x1 -> x0, blocking collectives: 118 us -> none  [local(): cum_all = lax.all_gather(cum_own[None], 'seq', axis=1, tiled=True)]
    pallas_call x0 -> x1, Pallas kernels: none -> 89.5 us  [local(): pl.pallas_call(body, out_shape=(jax.ShapeDtypeStruct((rows, width), F32),...]
    reduce_scatter x1 -> x0, waiting for transfers between devices: 73.7 us -> none  [local(): lax.psum_scatter(grad_full, 'seq', scatter_dimension=0, tiled=True)]
    another operation x4 -> x0, loops' own time: 43.1 us -> none  [the longest x2 42.4 us: prefix(): return lax.fori_loop(0, ahead, one, state)]
    dynamic_slice x64 -> x0, local copies, waits for them, and re-layouts: 36.9 us -> none  [the longest x63 36.9 us: one(): return combine(state, lax.dynamic_index_in_dim(gathered, source, 0, False))]
    dot_general x5 -> x0, matrix products: 8.2 us -> none  [the longest x2 2.65 us: score_block(): jnp.dot(query_rows, key_rows.T, preferred_element_type=jnp.float32)]
  transfers between devices with their start and end apart: 3 -> 0, of which waited for: 1 -> 0; matrix products, arithmetic and copies ran while one was open for 1% -> 0% of each run, Pallas kernels for 0% -> 0%
where the time goes in v1:
time: 97.5 us; the launch traced here: 97.2 us
  Pallas kernels  89.5 us (92%)
  local copies, waits for them, and re-layouts  5.9 us (6%)
  between operations  1.82 us (2%)
    pallas_call x1, Pallas kernels, local(): pl.pallas_call(body, out_shape=(jax.ShapeDtypeStruct((rows, width), F32),...  89.5 us
    unnamed x13, local copies, waits for them, and re-layouts  5.9 us

profile of v1, /device:TPU:8, one launch (start us, length us, event | category | flops | bytes accessed | tf_op | source)
XLA Modules:
  0.0 97.2 jit_solution(7255653731552813091)
XLA Ops:
  0.6 0.0 copy-start.4
  0.6 0.7 copy-done.4
  1.3 0.0 copy-start
  1.3 0.8 copy-done
  2.2 0.0 copy-start.1
  2.2 0.8 copy-done.1
  3.0 0.0 copy-start.2
  3.0 0.8 copy-done.2
  3.8 0.0 copy-start.3
  3.8 0.8 copy-done.3
  4.7 89.5 %shard_map.84 = (f32[256,128]{1,0:T(8,128)S(1)}, f32[256,128]{1,0:T(8,128)S(1)}, f32[1,256]{1,0:T(1,128)S(1)}, f32[1,128]{1,0:T(1,128)S(1)}) custom-call(bf16[256,128]{1,0:T(8,128)(2,1)S(1)} %bitcast.10, bf16[256,128]{1,0:T(8,128)(2,1)S(1)} %bitcast.11, bf16[256,128]{1,0:T(8,128)(2,1)S(1)} %bitcast.12, bf16[256,128]{1,0:T(8,128)(2,1)S(1)} %bitcast.13, ...), custom_call_target="tpu_custom_call" | custom-call | tf_op jit(solution)/shard_map/pallas_call | solution.py:515
  94.2 0.7 copy.13
  94.8 0.7 copy.14
  95.5 0.6 copy.15
Async XLA Ops:
  0.6 0.7 copy-start.4
  1.3 0.8 copy-start
  2.2 0.8 copy-start.1
  3.0 0.8 copy-start.2
  3.8 0.8 copy-start.3
